TPU v7x, 32 devices: a whole 2x2x4 slice. The times are simulated.
32 devices in a mesh: dp: 4 (over z), ctx: 8 (over y, x, core).
Axes of the slice: x: 2, y: 2, z: 4, core: 2. Of those that a mesh axis runs over, the one named last changes fastest.
Arguments:
- query_in: bfloat16 [4, 1024, 2048], P('dp', 'ctx'), may hold values from -6 to 6
- key_in: bfloat16 [4, 1024, 2048], P('dp', 'ctx'), may hold values from -6 to 6
- value_in: bfloat16 [4, 1024, 2048], P('dp', 'ctx'), may hold values from -6 to 6
- out_grad: bfloat16 [4, 1024, 2048], P('dp', 'ctx'), may hold values from -6 to 6
- log_decay: bfloat16 [4, 1024, 32], P('dp', 'ctx'), may hold values from -2 to 0, as said below
- doc_ids: int32 [4, 8], P('dp'), may hold values from 0 to 3, never falling along the last dimension, each value on 1 to 4 neighbouring positions
- norm_gain: float32 [2048], replicated, may hold values from 0.1 to 1.9
Outputs:
- query_grad: bfloat16 [4, 1024, 2048], P('dp', 'ctx')
- key_grad: bfloat16 [4, 1024, 2048], P('dp', 'ctx')
- value_grad: bfloat16 [4, 1024, 2048], P('dp', 'ctx')
- gain_grad: float32 [2048], replicated
Inputs may be any that keep to these rules, and one draw needn't show every extreme that they name: log_decay is never positive. Within a sequence doc_ids never fall; each of the 4 documents covers 1 to half of 8 blocks, and one covers exactly half of 8.
All inputs are finite; a program needn't handle non-finite values.
Results may differ from a plain program's by a relative error of at most 0.0061.
Values may be sent and summed in bfloat16 or wider, within the bound.
A program may use at most 192 MiB of HBM per device.

v0:
```python
import math

import jax
import jax.numpy as jnp
from jax import lax
from jax.sharding import PartitionSpec as P

BLOCK = 128


HIGHEST_PRECISION = lax.Precision.HIGHEST
EPSILON = 1e-05


def carried_in(value, axis, join, neutral, backward):
    count, mine = (lax.axis_size(axis), lax.axis_index(axis))
    pieces = jax.tree.map(lambda part: lax.all_gather(part, axis), value)
    if backward:
        pieces = jax.tree.map(lambda part: part[::-1], pieces)
        mine = count - 1 - mine
    running = jax.tree.map(
        lambda part, zero: jnp.full_like(part, 0) + jnp.asarray(zero, part.dtype), value, neutral
    )

    def step(position, running):
        longer = join(running, jax.tree.map(lambda part: part[position], pieces))
        return jax.tree.map(lambda new, old: jnp.where(position < mine, new, old), longer, running)

    return lax.fori_loop(0, count - 1, step, running)


def block_starts(doc_row):
    changed = (doc_row[1:] != doc_row[:-1]).astype(jnp.float32)
    return jnp.concatenate([jnp.ones((1,), jnp.float32), changed])


def combine_states(earlier, later):
    return (earlier[0] * later[0], later[0][:, None, None] * earlier[1] + later[1])


def decay_tables(log_rate, starts):
    nblocks = log_rate.shape[0]
    block_len = log_rate.shape[1]
    within = jnp.cumsum(log_rate, axis=1)
    block_total = within[:, -1]
    bounds = jnp.concatenate(
        [jnp.zeros((1, block_total.shape[1]), jnp.float32), jnp.cumsum(block_total, axis=0)], axis=0
    )
    counts = jnp.concatenate([jnp.zeros((1,), jnp.float32), jnp.cumsum(starts)])
    row_index = jnp.arange(nblocks + 1)[:, None]
    col_index = jnp.arange(nblocks)[None, :]
    forward_ok = (col_index + 1 <= row_index) & (counts[:, None] == counts[None, 1:])
    forward_mix = jnp.where(
        forward_ok[:, :, None],
        jnp.exp(jnp.minimum(bounds[:, None, :] - bounds[None, 1:, :], 0.0)),
        0.0,
    )
    reverse_ok = (col_index >= row_index) & (counts[None, :nblocks] == counts[:, None])
    reverse_mix = jnp.where(
        reverse_ok[:, :, None],
        jnp.exp(jnp.minimum(bounds[None, :nblocks, :] - bounds[:, None, :], 0.0)),
        0.0,
    )
    forward_seed = jnp.where((counts == 0.0)[:, None], jnp.exp(bounds), 0.0)
    reverse_seed = jnp.where(
        (counts == counts[nblocks])[:, None], jnp.exp(bounds[nblocks][None, :] - bounds), 0.0
    )
    keep_state = 1.0 - starts
    head_weight = jnp.exp(within) * keep_state[:, None, None]
    tail_weight = jnp.exp(block_total[:, None, :] - within)
    within_heads = jnp.moveaxis(within, 2, 1)
    log_gaps = within_heads[:, :, :, None] - within_heads[:, :, None, :]
    causal = jnp.arange(block_len)[:, None] >= jnp.arange(block_len)[None, :]
    intra_weight = jnp.where(causal[None, None], jnp.exp(jnp.minimum(log_gaps, 0.0)), 0.0)
    return (
        intra_weight,
        head_weight,
        tail_weight,
        forward_mix,
        reverse_mix,
        forward_seed,
        reverse_seed,
    )


def forward_local(query_blocks, key_blocks, value_blocks, tables):
    scores = jnp.einsum(
        "bthd,bshd->bhts", query_blocks, key_blocks, preferred_element_type=jnp.float32
    )
    block_probs = (scores * tables[0]).astype(jnp.bfloat16)
    keyed = (key_blocks.astype(jnp.float32) * tables[2][..., None]).astype(jnp.bfloat16)
    block_state = jnp.einsum(
        "bshd,bshe->bhde", keyed, value_blocks, preferred_element_type=jnp.float32
    )
    gathered = jnp.einsum("cbh,bhde->chde", tables[3], block_state, precision=HIGHEST_PRECISION)
    return (block_probs, gathered)


def attend_output(query_blocks, value_blocks, block_probs, head_weight, states):
    local_part = jnp.einsum(
        "bhts,bshd->bthd", block_probs, value_blocks, preferred_element_type=jnp.float32
    )
    weighted = (query_blocks.astype(jnp.float32) * head_weight[..., None]).astype(jnp.bfloat16)
    carried = jnp.einsum(
        "bthd,bhde->bthe",
        weighted,
        states[:-1].astype(jnp.bfloat16),
        preferred_element_type=jnp.float32,
    )
    return local_part + carried


def norm_backward(attn_flat, grad_flat, gain_part, square_sum, cross_sum, count):
    inv_rms = lax.rsqrt(square_sum / count + EPSILON)
    grad_input = (
        inv_rms[:, None] * gain_part[None, :] * grad_flat
        - (inv_rms * inv_rms * inv_rms * cross_sum / count)[:, None] * attn_flat
    )
    gain_local = jnp.sum(grad_flat * attn_flat * inv_rms[:, None], axis=0)
    return (grad_input.astype(jnp.bfloat16), gain_local)


def backward_summary(query_blocks, grad_blocks, head_weight, reverse_mix):
    queried = (query_blocks.astype(jnp.float32) * head_weight[..., None]).astype(jnp.bfloat16)
    back_block = jnp.einsum(
        "bthd,bthe->bhde", queried, grad_blocks, preferred_element_type=jnp.float32
    )
    return jnp.einsum("jbh,bhde->jhde", reverse_mix, back_block, precision=HIGHEST_PRECISION)


def backward_local(
    query_blocks, key_blocks, value_blocks, grad_blocks, block_probs, tables, states, after_states
):
    intra_weight, head_weight, tail_weight = (tables[0], tables[1], tables[2])
    grad_scores = jnp.einsum(
        "bthd,bshd->bhts", grad_blocks, value_blocks, preferred_element_type=jnp.float32
    )
    grad_scores = (grad_scores * intra_weight).astype(jnp.bfloat16)
    weighted_grad = (grad_blocks.astype(jnp.float32) * head_weight[..., None]).astype(jnp.bfloat16)
    grad_query = jnp.einsum(
        "bhts,bshd->bthd", grad_scores, key_blocks, preferred_element_type=jnp.float32
    )
    grad_query = grad_query + jnp.einsum(
        "bthe,bhde->bthd",
        weighted_grad,
        states[:-1].astype(jnp.bfloat16),
        preferred_element_type=jnp.float32,
    )
    later = after_states[1:].astype(jnp.bfloat16)
    grad_key = jnp.einsum(
        "bhts,bthd->bshd", grad_scores, query_blocks, preferred_element_type=jnp.float32
    )
    grad_key = grad_key + tail_weight[..., None] * jnp.einsum(
        "bshe,bhde->bshd", value_blocks, later, preferred_element_type=jnp.float32
    )
    grad_value = jnp.einsum(
        "bhts,bthe->bshe", block_probs, grad_blocks, preferred_element_type=jnp.float32
    )
    grad_value = grad_value + tail_weight[..., None] * jnp.einsum(
        "bshd,bhde->bshe", key_blocks, later, preferred_element_type=jnp.float32
    )
    return (
        grad_query.astype(jnp.bfloat16),
        grad_key.astype(jnp.bfloat16),
        grad_value.astype(jnp.bfloat16),
    )


def one_sequence(query_seq, key_seq, value_seq, grad_seq, decay_seq, doc_row, norm_gain):
    local_len = query_seq.shape[0]
    feature_width = query_seq.shape[1]
    head_count = decay_seq.shape[1]
    head_dim = feature_width // head_count
    starts_all = block_starts(doc_row)
    nblocks = local_len // BLOCK
    starts = lax.dynamic_slice_in_dim(starts_all, lax.axis_index("ctx") * nblocks, nblocks)
    query_blocks = query_seq.reshape(nblocks, BLOCK, head_count, head_dim)
    key_blocks = key_seq.reshape(nblocks, BLOCK, head_count, head_dim)
    value_blocks = value_seq.reshape(nblocks, BLOCK, head_count, head_dim)
    log_rate = decay_seq.astype(jnp.float32).reshape(nblocks, BLOCK, head_count)
    tables = decay_tables(log_rate, starts)
    block_probs, gathered = forward_local(query_blocks, key_blocks, value_blocks, tables)
    seed_weight = tables[5]
    device_decay = seed_weight[-1]
    identity = (jnp.ones_like(device_decay), jnp.zeros_like(gathered[-1]))
    incoming = carried_in((device_decay, gathered[-1]), "ctx", combine_states, identity, False)
    states = gathered + seed_weight[:, :, None, None] * incoming[1][None]
    attn_blocks = attend_output(query_blocks, value_blocks, block_probs, tables[1], states)
    attn_flat = attn_blocks.reshape(local_len, feature_width)
    grad_flat = grad_seq.astype(jnp.float32)
    square_sum = jnp.sum(attn_flat * attn_flat, axis=1)
    cross_sum = jnp.sum(attn_flat * norm_gain[None, :] * grad_flat, axis=1)
    grad_input, gain_terms = norm_backward(
        attn_flat, grad_flat, norm_gain, square_sum, cross_sum, feature_width
    )
    grad_blocks = grad_input.reshape(nblocks, BLOCK, head_count, head_dim)
    back_gathered = backward_summary(query_blocks, grad_blocks, tables[1], tables[4])
    outgoing = carried_in((device_decay, back_gathered[0]), "ctx", combine_states, identity, True)
    after_states = back_gathered + tables[6][:, :, None, None] * outgoing[1][None]
    grad_query, grad_key, grad_value = backward_local(
        query_blocks,
        key_blocks,
        value_blocks,
        grad_blocks,
        block_probs,
        tables,
        states,
        after_states,
    )
    query_grad = grad_query.reshape(local_len, feature_width)
    key_grad = grad_key.reshape(local_len, feature_width)
    value_grad = grad_value.reshape(local_len, feature_width)
    return (query_grad, key_grad, value_grad, gain_terms)


def body(query_in, key_in, value_in, out_grad, log_decay, doc_ids, norm_gain):
    row_count = query_in.shape[0]
    query_row, key_row, value_row, gain_row = one_sequence(
        query_in[0], key_in[0], value_in[0], out_grad[0], log_decay[0], doc_ids[0], norm_gain
    )
    query_list = [query_row]
    key_list = [key_row]
    value_list = [value_row]
    seq_len = query_in.shape[1] * lax.axis_size("ctx")
    total_tokens = lax.axis_size("dp") * row_count * seq_len
    gain_grad = lax.psum(gain_row, ("dp", "ctx")) / math.sqrt(total_tokens)
    return (jnp.stack(query_list), jnp.stack(key_list), jnp.stack(value_list), gain_grad)


def solution(mesh):
    placed = (
        P("dp", "ctx", None),
        P("dp", "ctx", None),
        P("dp", "ctx", None),
        P("dp", "ctx", None),
        P("dp", "ctx", None),
        P("dp", None),
        P(),
    )
    return jax.shard_map(
        body,
        mesh=mesh,
        in_specs=placed,
        out_specs=(P("dp", "ctx", None), P("dp", "ctx", None), P("dp", "ctx", None), P()),
        check_vma=False,
    )
```

profile of v0, /device:TPU:0, one launch (start us, length us, event | category | flops | bytes accessed | tf_op | source)
XLA Modules:
  0.0 180.1 jit_solution(14923864551213685095)
XLA Ops:
  13.8 1.5 copy.81
  19.0 2.0 %copy.76 = bf16[1,128,2048]{1,2,0:T(8,128)(2,1)} copy(bf16[1,128,2048]{2,1,0:T(8,128)(2,1)} %param.11) | data formatting | bytes 1048576 | tf_op args[0]
  22.5 10.2 %all-gather = f32[8,1,32]{2,1,0:T(1,128)S(1)} all-gather(f32[1,1,32]{2,1,0:T(1,128)S(1)} %get-tuple-element.287), channel_id=1, replica_groups=mesh['dp'=4,'ctx'=8] {'ctx'}, dimensions={0}, use_global_device_ids=true | all-gather | bytes 1152 | tf_op jit(solution)/shard_map/all_gather | solution.py:17
  32.7 2.0 %multiply_convert_fusion.1 = bf16[32,128,128]{2,1,0:T(8,128)(2,1)S(1)} fusion(bf16[128,32,64]{0,2,1:T(8,128)(2,1)} %bitcast.139, bf16[128,32,64]{0,2,1:T(8,128)(2,1)S(1)} %bitcast.136, f32[32,128]{1,0:T(8,128)S(1)} %copy.79, pred[128,128]{1,0:T(8,128)(4,1)S(1)} %iota_compare_fusion), kind=kOutput, calls=%fused_computation.9 | convolution fusion | flops 69730304 | bytes 2129920 | tf_op jit(solution)/shard_map/bthd,bshd->bhts/dot_general | solution.py:87
  35.7 1.8 convolution_bitcast_fusion.5
  37.4 38.8 %all-gather.4.cloned.1.call-done = f32[8,32,64,64]{3,2,1,0:T(8,128)} async-done(((f32[1,32,64,64]{3,2,1,0:T(8,128)}), f32[8,32,64,64]{3,2,1,0:T(8,128)}) %all-gather.4.cloned.1.call-update) | async-done | bytes 4194320 | tf_op jit(solution)/shard_map/all_gather | solution.py:17
  76.2 10.5 %while.28 = (s32[]{:T(128)}, f32[32,64,64]{2,1,0:T(8,128)S(1)}, s32[]{:T(128)}, f32[8,32]{1,0:T(8,128)S(1)}, f32[8,32,64,64]{3,2,1,0:T(8,128)}, /*index=5*/s32[]{:T(128)}, s32[]{:T(128)}) while((s32[]{:T(128)}, f32[32,64,64]{2,1,0:T(8,128)S(1)}, s32[]{:T(128)}, f32[8,32]{1,0:T(8,128)S(1)}, f32[8,32,64,64]{3,2,1,0:T(8,128)}, ...), condition=%wide.region_2.3_spmd.clone, body=%wide.region_1.2_spmd.clone.sunk | while | flops 524292 | bytes 1573353 | solution.py:29
  77.7 1.5 fusion.58
  79.2 1.5 fusion.58
  80.7 1.5 fusion.58
  82.2 1.5 fusion.58
  83.7 1.5 fusion.58
  85.2 1.5 fusion.58
  88.0 1.8 %fusion.15 = bf16[32,64,64]{1,2,0:T(8,128)(2,1)S(1)} fusion(f32[2,32,64,64]{2,3,1,0:T(8,128)} %copy-done, f32[32,64,64]{1,2,0:T(8,128)} %copy.85, f32[1,32]{1,0:T(1,128)S(1)} %get-tuple-element.286), kind=kLoop, calls=%fused_computation.40 | loop fusion | flops 393216 | bytes 1310848 | tf_op jit(solution)/shard_map/reshape.34
  93.3 2.2 %multiply_convert_fusion = bf16[32,128,128]{2,1,0:T(8,128)(2,1)S(1)} fusion(bf16[128,32,64]{0,2,1:T(8,128)(2,1)} %bitcast.133, f32[32,128]{1,0:T(8,128)S(1)} %copy.79, pred[128,128]{1,0:T(8,128)(4,1)S(1)} %iota_compare_fusion, bf16[1,128,32,64]{1,3,2,0:T(8,128)(2,1)} %copy-done.6), kind=kOutput, calls=%fused_computation.7 | convolution fusion | flops 69730304 | bytes 2129920 | tf_op jit(solution)/shard_map/bthd,bshd->bhts/dot_general | solution.py:135
  98.3 2.0 %copy.89 = bf16[1,128,2048]{2,1,0:T(8,128)(2,1)} copy(bf16[1,128,2048]{1,2,0:T(8,128)(2,1)} %bitcast.143) | data formatting | bytes 1048576
  100.4 40.0 %psum.7 = f32[2048]{0:T(1024)S(1)} all-reduce(f32[2048]{0:T(1024)S(1)} %reduce_sum.32), channel_id=1, replica_groups=mesh['dp'=4,'ctx'=8] {'dp','ctx'}, use_global_device_ids=true, to_apply=%region_8.9 | all-reduce | flops 2048 | bytes 16384 | tf_op jit(solution)/shard_map/psum | solution.py:226
  140.9 8.3 %all-gather.6.cloned.1.call-done = f32[8,32,64,64]{3,2,1,0:T(8,128)} async-done(((f32[1,32,64,64]{3,2,1,0:T(8,128)}), f32[8,32,64,64]{3,2,1,0:T(8,128)}) %all-gather.6.cloned.1.call-update) | async-done | bytes 4194320 | tf_op jit(solution)/shard_map/all_gather | solution.py:17
  149.2 8.3 %rev.7 = f32[8,32,64,64]{3,2,1,0:T(8,128)} reverse(f32[8,32,64,64]{3,2,1,0:T(8,128)} %all-gather.6.cloned.1.call-done), dimensions={0} | reverse | bytes 8388608 | tf_op jit(solution)/shard_map/rev | solution.py:19
  157.5 10.5 %while.29 = (s32[]{:T(128)}, f32[32,64,64]{2,1,0:T(8,128)S(1)}, s32[]{:T(128)}, f32[8,32]{1,0:T(8,128)S(1)}, f32[8,32,64,64]{3,2,1,0:T(8,128)}, /*index=5*/s32[]{:T(128)}, s32[]{:T(128)}) while((s32[]{:T(128)}, f32[32,64,64]{2,1,0:T(8,128)S(1)}, s32[]{:T(128)}, f32[8,32]{1,0:T(8,128)S(1)}, f32[8,32,64,64]{3,2,1,0:T(8,128)}, ...), condition=%wide.region_6.7_spmd.clone, body=%wide.region_5.6_spmd.clone.sunk | while | flops 524292 | bytes 1573353 | solution.py:29
  160.5 1.5 fusion.59
  162.0 1.5 fusion.59
  163.5 1.5 fusion.59
  165.0 1.5 fusion.59
  (105 shorter events, 31.3 us)
Async XLA Ops:
  7.2 69.0 %all-gather.4.cloned.1.call-start = ((), (), s32[]{:S(2)}) async-start(), calls=%async_computation | async-start | bytes 9437184 | tf_op jit(solution)/shard_map/all_gather | solution.py:17
  13.8 18.9 %copy-start.3 = (bf16[1,128,2048]{1,2,0:T(8,128)(2,1)}, bf16[1,128,2048]{1,2,0:T(8,128)(2,1)S(1)}, u32[]{:S(2)}) copy-start(bf16[1,128,2048]{1,2,0:T(8,128)(2,1)S(1)} %copy.77) | copy-start | bytes 1572868
  15.3 19.3 %copy-start.1 = (bf16[1,128,2048]{1,2,0:T(8,128)(2,1)}, bf16[1,128,2048]{1,2,0:T(8,128)(2,1)S(1)}, u32[]{:S(2)}) copy-start(bf16[1,128,2048]{1,2,0:T(8,128)(2,1)S(1)} %copy.81) | copy-start | bytes 1572868
  16.1 1.4 copy-start
  18.9 3.5 %copy-start.18 = (f32[2048]{0:T(1024)S(1)}, f32[2048]{0:T(1024)}, u32[]{:S(2)}) copy-start(f32[2048]{0:T(1024)} %param.17) | copy-start | bytes 24580
  18.9 130.3 %all-gather.6.cloned.1.call-start = ((), (), s32[]{:S(2)}) async-start(), calls=%async_computation.1 | async-start | bytes 9437184 | tf_op jit(solution)/shard_map/all_gather | solution.py:17
  34.7 1.0 copy-start.13
  86.7 3.2 %copy-start.9 = (bf16[1,128,2048]{1,2,0:T(8,128)(2,1)S(1)}, bf16[1,128,2048]{1,2,0:T(8,128)(2,1)}, u32[]{:S(2)}) copy-start(bf16[1,128,2048]{1,2,0:T(8,128)(2,1)} %copy.76) | copy-start | bytes 1572868
  88.0 1.9 %copy-start.17 = (f32[32,64,128]{2,1,0:T(8,128)S(1)}, f32[32,64,128]{2,1,0:T(8,128)}, u32[]{:S(2)}) copy-start(f32[32,64,128]{2,1,0:T(8,128)} %convolution_bitcast_fusion.5) | copy-start | bytes 3145732
  89.9 1.1 copy-start.11
  91.4 0.8 copy-start.6
  93.3 2.2 %copy-start.4 = (bf16[1,128,2048]{1,2,0:T(8,128)(2,1)S(1)}, bf16[1,128,2048]{1,2,0:T(8,128)(2,1)}, u32[]{:S(2)}) copy-start(bf16[1,128,2048]{1,2,0:T(8,128)(2,1)} %copy-done.3) | copy-start | bytes 1572868
  95.5 2.8 %copy-start.15 = (bf16[32,128,128]{2,1,0:T(8,128)(2,1)}, bf16[32,128,128]{2,1,0:T(8,128)(2,1)S(1)}, u32[]{:S(2)}) copy-start(bf16[32,128,128]{2,1,0:T(8,128)(2,1)S(1)} %multiply_convert_fusion) | copy-start | bytes 3145732
  95.5 1.4 copy-start.7
  95.5 1.6 copy-start.12
  168.0 1.0 copy-start.5
  168.0 1.4 copy-start.2
  169.0 1.1 copy-start.8
  169.0 1.4 copy-start.14
  170.4 1.4 copy-start.10
  170.4 1.4 copy-start.16
Sparse Core Ops, SparseCore 0:
  19.1 57.0 all-gather.3
  93.4 55.7 all-gather.5
where the time goes:
time: 181 us; the launch traced here: 180 us
  blocking collectives  50.2 us (28%)
  waiting for transfers between devices  47 us (26%)
  local copies, waits for them, and re-layouts  29 us (16%)
  other arithmetic  27.8 us (15%)
  between operations  15 us (8%)
  matrix products  10.6 us (6%)
    all_gather x2, waiting for transfers between devices, carried_in(): pieces = jax.tree.map(lambda part: lax.all_gather(part, axis), value)  47 us
    psum x1, blocking collectives, body(): gain_grad = lax.psum(gain_row, ('dp', 'ctx')) / math.sqrt(total_tokens)  40 us
    select_n x14, other arithmetic, step(): jnp.where(position < mine, new, old)  20.5 us
    unnamed x44, local copies, waits for them, and re-layouts  13.9 us
    all_gather x1, blocking collectives, carried_in(): pieces = jax.tree.map(lambda part: lax.all_gather(part, axis), value)  10.2 us
    rev x2, local copies, waits for them, and re-layouts, carried_in(): pieces = jax.tree.map(lambda part: part[::-1], pieces)  8.29 us
  transfers between devices with their start and end apart: 2, of which 2 were waited for; matrix products, arithmetic and copies ran while one was open for 8% of the time, Pallas kernels for 0%

commit v1 on v0

v1 whole, which is shorter than its diff:
```python
import functools
import math

import jax
import jax.numpy as jnp
from jax import lax
from jax.experimental import pallas as pl
from jax.experimental.pallas import tpu as pltpu
from jax.sharding import PartitionSpec as P

EPSILON = 1e-05
MESH = pl.DeviceIdType.MESH
UNROLL = 4
F32 = jnp.float32
BF16 = jnp.bfloat16


def dot(left, right, left_dim, right_dim):
    return lax.dot_general(
        left, right, (((left_dim,), (right_dim,)), ((), ())), preferred_element_type=F32
    )


def kernel(
    ctx_count, dp_count, tokens,
    q_ref, k_ref, v_ref, g_ref, decay_ref, doc_ref, gain_ref,
    dq_ref, dk_ref, dv_ref, gain_out_ref,
    rows_s, weight_s, head_s, tail_s, probs_s, attn_s, grad_s, qw_s, dk_s, dv_s,
    carry_all, term_out, term_in, state_out, state_in,
    back_term_out, back_term_in, back_out, back_in,
    gain_all, gain_mid, gain_dp,
    send_sem, recv_sem, gain_send_sem, gain_recv_sem,
):
    length, width = q_ref.shape
    lanes = 128
    half = lanes // 2
    pairs = width // lanes
    chunk = pairs * half // ctx_count
    me = lax.axis_index("ctx")
    row_me = lax.axis_index("dp")

    barrier = pltpu.get_barrier_semaphore()
    for j in range(1, ctx_count):
        other = lax.rem(me + j, ctx_count)
        pl.semaphore_signal(barrier, inc=1, device_id={"ctx": other}, device_id_type=MESH)
    for j in range(1, dp_count):
        other = lax.rem(row_me + j, dp_count)
        pl.semaphore_signal(barrier, inc=1, device_id={"dp": other}, device_id_type=MESH)

    left_half = lax.broadcasted_iota(jnp.int32, (1, lanes), 1) < half

    def cols(pair):
        return pl.ds(pl.multiple_of(pair * lanes, lanes), lanes)

    def packed_rows(pair):
        return pl.ds(pl.multiple_of(pair * half, half), half)

    def pick(first, second):
        return jnp.where(left_half, first, second)

    def stacked(block):
        zero = jnp.zeros_like(block)
        return jnp.concatenate([pick(block, zero), pick(zero, block)], axis=0)

    def packed(full, size):
        return pick(full[:size], full[size:])

    def over_pairs(first, last, fn, init=0):
        return lax.fori_loop(first, last, fn, init, unroll=UNROLL)

    step_row = lax.broadcasted_iota(jnp.int32, (length, length), 0)
    step_col = lax.broadcasted_iota(jnp.int32, (length, length), 1)
    upto = jnp.where(step_row <= step_col, 1.0, 0.0).astype(BF16)
    rows_s[...] = dot(decay_ref[...], upto, 0, 0)

    same_doc = doc_ref[0, me] == doc_ref[0, jnp.maximum(me - 1, 0)]
    keep = jnp.where(same_doc, 1.0, 0.0) * jnp.where(me == 0, 0.0, 1.0)

    def column(head):
        row = rows_s[pl.ds(head, 1), :]
        return row, jnp.transpose(jnp.broadcast_to(row, (length, lanes)))

    def terms_step(pair, _):
        _, first = column(2 * pair)
        _, second = column(2 * pair + 1)
        within = pick(first, second)
        total = within[length - 1 :, :]
        tail = jnp.exp(total - within)
        tail_s[:, cols(pair)] = tail
        head_s[:, cols(pair)] = jnp.exp(within) * keep
        carry_all[me, pl.ds(pair, 1), :] = jnp.exp(total) * keep
        keyed = (k_ref[:, cols(pair)].astype(F32) * tail).astype(BF16)
        full = dot(keyed, v_ref[:, cols(pair)], 0, 0)
        term_out[packed_rows(pair), :] = packed(full, half).astype(BF16)
        return 0

    over_pairs(0, pairs, terms_step)
    pl.semaphore_wait(barrier, ctx_count - 1 + dp_count - 1)

    def piece(index):
        return pl.ds(pl.multiple_of(index * chunk, chunk), chunk)

    def to_all(phase, source, target):
        copies = []
        for j in range(1, ctx_count):
            other = lax.rem(me + j, ctx_count)
            copies.append(
                pltpu.make_async_remote_copy(
                    src_ref=source(other),
                    dst_ref=target(),
                    send_sem=send_sem.at[phase, j],
                    recv_sem=recv_sem.at[phase, j],
                    device_id={"ctx": other},
                    device_id_type=MESH,
                )
            )
        for copy in copies:
            copy.start()
        return copies

    def finish(copies):
        for copy in copies:
            copy.wait()

    def combine(term_ref, out_ref, backward):
        per = max(chunk // half, 1)
        size = min(chunk, half)
        running = [jnp.zeros((size, lanes), F32) for _ in range(per)]
        order = range(ctx_count - 1, -1, -1) if backward else range(ctx_count)
        for block in order:
            for i in range(per):
                pair = lax.div(me * chunk, half) + i
                out_ref[block, i * size : (i + 1) * size, :] = running[i].astype(BF16)
                carry = carry_all[block, pl.ds(pair, 1), :]
                running[i] = carry * running[i] + term_ref[
                    block, i * size : (i + 1) * size, :
                ].astype(F32)

    def exchange_terms(phase, out_ref, in_ref):
        in_ref[me] = out_ref[piece(me), :]
        return to_all(phase, lambda other: out_ref.at[piece(other), :], lambda: in_ref.at[me])

    def exchange_states(phase, out_ref, in_ref):
        in_ref[piece(me), :] = out_ref[me]
        return to_all(phase, lambda other: out_ref.at[other], lambda: in_ref.at[piece(me), :])

    carry_copies = to_all(0, lambda other: carry_all.at[me], lambda: carry_all.at[me])
    term_copies = exchange_terms(1, term_out, term_in)

    causal = step_row >= step_col

    def local_step(pair, _):
        weights = []
        for head in (2 * pair, 2 * pair + 1):
            row, col = column(head)
            weights.append(jnp.where(causal, jnp.exp(jnp.minimum(col - row, 0.0)), 0.0))
        weight = jnp.concatenate(weights, axis=1)
        weight_s[pair] = weight
        scores = dot(q_ref[:, cols(pair)], stacked(k_ref[:, cols(pair)]), 1, 1)
        probs = (scores * weight).astype(BF16)
        probs_s[pair] = probs
        attn_s[:, cols(pair)] = dot(probs, stacked(v_ref[:, cols(pair)]), 1, 0)
        qw_s[:, cols(pair)] = (q_ref[:, cols(pair)].astype(F32) * head_s[:, cols(pair)]).astype(BF16)
        return 0

    over_pairs(0, pairs // 2, local_step)
    finish(carry_copies)
    finish(term_copies)
    combine(term_in, state_out, False)
    state_copies = exchange_states(2, state_out, state_in)
    over_pairs(pairs // 2, pairs, local_step)
    finish(state_copies)

    def attend_step(pair, sums):
        square, cross = sums
        carried = dot(qw_s[:, cols(pair)], stacked(state_in[packed_rows(pair), :]), 1, 0)
        attn = attn_s[:, cols(pair)] + carried
        attn_s[:, cols(pair)] = attn
        scaled = gain_ref[:, cols(pair)] * g_ref[:, cols(pair)].astype(F32)
        return square + attn * attn, cross + attn * scaled

    zero = jnp.zeros((length, lanes), F32)
    square, cross = over_pairs(0, pairs, attend_step, (zero, zero))
    inv_rms = lax.rsqrt(jnp.sum(square, axis=1, keepdims=True) / width + EPSILON)
    shift = inv_rms * inv_rms * inv_rms * jnp.sum(cross, axis=1, keepdims=True) / width

    def norm_step(pair, _):
        grad_out = g_ref[:, cols(pair)].astype(F32)
        attn = attn_s[:, cols(pair)]
        grad = inv_rms * (gain_ref[:, cols(pair)] * grad_out) - shift * attn
        grad = grad.astype(BF16)
        grad_s[:, cols(pair)] = grad
        full = dot(qw_s[:, cols(pair)], grad, 0, 0)
        back_term_out[packed_rows(pair), :] = packed(full, half).astype(BF16)
        gain_all[me, :, cols(pair)] = jnp.sum(grad_out * attn * inv_rms, axis=0, keepdims=True)
        return 0

    over_pairs(0, pairs, norm_step)
    back_term_copies = exchange_terms(3, back_term_out, back_term_in)
    gain_copies = to_all(4, lambda other: gain_all.at[me], lambda: gain_all.at[me])

    def grads_step(pair, _):
        grad = grad_s[:, cols(pair)]
        scores = dot(grad, stacked(v_ref[:, cols(pair)]), 1, 1)
        scores = (scores * weight_s[pair]).astype(BF16)
        weighted = (grad.astype(F32) * head_s[:, cols(pair)]).astype(BF16)
        dq = dot(scores, stacked(k_ref[:, cols(pair)]), 1, 0)
        dq = dq + dot(weighted, stacked(state_in[packed_rows(pair), :]), 1, 1)
        dq_ref[:, cols(pair)] = dq.astype(BF16)
        dk_s[:, cols(pair)] = packed(dot(scores, q_ref[:, cols(pair)], 0, 0), length)
        dv_s[:, cols(pair)] = packed(dot(probs_s[pair], grad, 0, 0), length)
        return 0

    over_pairs(0, pairs // 2, grads_step)
    finish(back_term_copies)
    combine(back_term_in, back_out, True)
    back_copies = exchange_states(5, back_out, back_in)
    finish(gain_copies)
    gain_ctx = gain_all[0]
    for block in range(1, ctx_count):
        gain_ctx = gain_ctx + gain_all[block]
    gain_mid[...] = gain_ctx
    dp_copies = []
    for j in range(1, dp_count):
        other = lax.rem(row_me + j, dp_count)
        dp_copies.append(
            pltpu.make_async_remote_copy(
                src_ref=gain_mid,
                dst_ref=gain_dp.at[row_me],
                send_sem=gain_send_sem.at[j],
                recv_sem=gain_recv_sem.at[j],
                device_id={"dp": other},
                device_id_type=MESH,
            )
        )
    for copy in dp_copies:
        copy.start()
    gain_dp[row_me] = gain_ctx
    over_pairs(pairs // 2, pairs, grads_step)
    finish(back_copies)

    def last_step(pair, _):
        back = stacked(back_in[packed_rows(pair), :])
        tail = tail_s[:, cols(pair)]
        dk = dk_s[:, cols(pair)] + tail * dot(v_ref[:, cols(pair)], back, 1, 1)
        dv = dv_s[:, cols(pair)] + tail * dot(k_ref[:, cols(pair)], back, 1, 0)
        dk_ref[:, cols(pair)] = dk.astype(BF16)
        dv_ref[:, cols(pair)] = dv.astype(BF16)
        return 0

    over_pairs(0, pairs, last_step)
    finish(dp_copies)
    gain_total = gain_dp[0]
    for row in range(1, dp_count):
        gain_total = gain_total + gain_dp[row]
    gain_out_ref[...] = gain_total / math.sqrt(tokens)


def body(query_in, key_in, value_in, out_grad, log_decay, doc_ids, norm_gain):
    _, length, width = query_in.shape
    ctx_count, dp_count = lax.axis_size("ctx"), lax.axis_size("dp")
    heads = log_decay.shape[2]
    pairs = heads // 2
    lanes = 128
    chunk = pairs * 64 // ctx_count
    tokens = dp_count * ctx_count * query_in.shape[0] * length
    flat = jax.ShapeDtypeStruct((length, width), BF16)
    vmem = pl.BlockSpec(memory_space=pltpu.VMEM)
    wide, narrow = pltpu.VMEM((length, width), F32), pltpu.VMEM((length, width), BF16)
    whole_state = pltpu.VMEM((pairs * 64, lanes), BF16)
    pieces = pltpu.VMEM((ctx_count, chunk, lanes), BF16)
    dq, dk, dv, gain_grad = pl.pallas_call(
        functools.partial(kernel, ctx_count, dp_count, tokens),
        out_shape=(flat, flat, flat, jax.ShapeDtypeStruct((1, width), F32)),
        in_specs=[vmem] * 5 + [pl.BlockSpec(memory_space=pltpu.SMEM), vmem],
        out_specs=(vmem,) * 4,
        scratch_shapes=[
            pltpu.VMEM((heads, length), F32),
            pltpu.VMEM((pairs, length, 2 * length), F32),
            wide,
            wide,
            pltpu.VMEM((pairs, length, 2 * length), BF16),
            wide,
            narrow,
            narrow,
            wide,
            wide,
            pltpu.VMEM((ctx_count, pairs, lanes), F32),
            whole_state,
            pieces,
            pieces,
            whole_state,
            whole_state,
            pieces,
            pieces,
            whole_state,
            pltpu.VMEM((ctx_count, 1, width), F32),
            pltpu.VMEM((1, width), F32),
            pltpu.VMEM((dp_count, 1, width), F32),
            pltpu.SemaphoreType.DMA((6, ctx_count)),
            pltpu.SemaphoreType.DMA((6, ctx_count)),
            pltpu.SemaphoreType.DMA((dp_count,)),
            pltpu.SemaphoreType.DMA((dp_count,)),
        ],
        compiler_params=pltpu.CompilerParams(
            collective_id=0, has_side_effects=True, vmem_limit_bytes=40 * 1024 * 1024
        ),
    )(
        query_in[0], key_in[0], value_in[0], out_grad[0], log_decay[0], doc_ids,
        norm_gain.reshape(1, width),
    )
    return dq[None], dk[None], dv[None], gain_grad[0]


def solution(mesh):
    seq = P("dp", "ctx", None)
    return jax.shard_map(
        body,
        mesh=mesh,
        in_specs=(seq, seq, seq, seq, seq, P("dp", None), P()),
        out_specs=(seq, seq, seq, P()),
        check_vma=False,
    )
```

time: 181 us -> 39.1 us (0.22)
  blocking collectives: 50.2 us -> 0 us
  waiting for transfers between devices: 47 us -> 0 us
  Pallas kernels: 0 us -> 29.4 us
  other arithmetic: 27.8 us -> 0 us
  local copies, waits for them, and re-layouts: 29 us -> 8.61 us
  between operations: 15 us -> 0.66 us
  matrix products: 10.6 us -> 0 us
    all_gather x2 -> x0, waiting for transfers between devices: 47 us -> none  [carried_in(): pieces = jax.tree.map(lambda part: lax.all_gather(part, axis), value)]
    psum x1 -> x0, blocking collectives: 40 us -> none  [body(): gain_grad = lax.psum(gain_row, ('dp', 'ctx')) / math.sqrt(total_tokens)]
    pallas_call x0 -> x1, Pallas kernels: none -> 29.4 us  [body(): pl.pallas_call(functools.partial(kernel, ctx_count, dp_count, tokens), ou...]
    select_n x15 -> x0, other arithmetic: 20.5 us -> none  [the longest x14 20.5 us: step(): jnp.where(position < mine, new, old)]
    dot_general x12 -> x0, matrix products: 10.6 us -> none  [the longest x1 2.2 us: backward_local(): jnp.einsum('bthd,bshd->bhts', grad_blocks, value_blocks, preferred_elemen...]
    all_gather x1 -> x0, blocking collectives: 10.2 us -> none  [carried_in(): pieces = jax.tree.map(lambda part: lax.all_gather(part, axis), value)]
    rev x2 -> x0, local copies, waits for them, and re-layouts: 8.29 us -> none  [carried_in(): pieces = jax.tree.map(lambda part: part[::-1], pieces)]
    unnamed x44 -> x19, local copies, waits for them, and re-layouts: 13.9 us -> 8.61 us
  transfers between devices with their start and end apart: 2 -> 0, of which waited for: 2 -> 0; matrix products, arithmetic and copies ran while one was open for 8% -> 0% of each run, Pallas kernels for 0% -> 0%
where the time goes in v1:
time: 39.1 us; the launch traced here: 38.7 us
  Pallas kernels  29.4 us (75%)
  local copies, waits for them, and re-layouts  8.61 us (22%)
  between operations  0.66 us (2%)
    pallas_call x1, Pallas kernels, body(): pl.pallas_call(functools.partial(kernel, ctx_count, dp_count, tokens), ou...  29.4 us
    unnamed x19, local copies, waits for them, and re-layouts  8.61 us

profile of v1, /device:TPU:0, one launch (start us, length us, event | category | flops | bytes accessed | tf_op | source)
XLA Modules:
  0.0 38.7 jit_solution(5710817585899432612)
XLA Ops:
  0.6 0.0 copy-start.6
  0.6 0.7 %copy-done.6 = bf16[1,128,32]{1,2,0:T(8,128)(2,1)S(1)} copy-done((bf16[1,128,32]{1,2,0:T(8,128)(2,1)S(1)}, bf16[1,128,32]{1,2,0:T(8,128)(2,1)}, u32[]{:S(2)}) %copy-start.6) | copy-done | bytes 8216
  1.3 0.0 copy-start.4
  1.3 0.1 copy.11
  1.4 0.0 copy-start.5
  1.5 0.6 %copy-done.4 = f32[2048]{0:T(1024)S(1)} copy-done((f32[2048]{0:T(1024)S(1)}, f32[2048]{0:T(1024)}, u32[]{:S(2)}) %copy-start.4) | copy-done | bytes 8216
  2.0 0.1 copy-done.5
  2.1 0.0 copy-start
  2.1 1.0 %copy-done = bf16[1,128,2048]{2,1,0:T(8,128)(2,1)S(1)} copy-done((bf16[1,128,2048]{2,1,0:T(8,128)(2,1)S(1)}, bf16[1,128,2048]{2,1,0:T(8,128)(2,1)}, u32[]{:S(2)}) %copy-start) | copy-done | bytes 524312
  3.2 0.0 copy-start.1
  3.2 1.0 %copy-done.1 = bf16[1,128,2048]{2,1,0:T(8,128)(2,1)S(1)} copy-done((bf16[1,128,2048]{2,1,0:T(8,128)(2,1)S(1)}, bf16[1,128,2048]{2,1,0:T(8,128)(2,1)}, u32[]{:S(2)}) %copy-start.1) | copy-done | bytes 524312
  4.2 0.0 copy-start.2
  4.2 1.0 %copy-done.2 = bf16[1,128,2048]{2,1,0:T(8,128)(2,1)S(1)} copy-done((bf16[1,128,2048]{2,1,0:T(8,128)(2,1)S(1)}, bf16[1,128,2048]{2,1,0:T(8,128)(2,1)}, u32[]{:S(2)}) %copy-start.2) | copy-done | bytes 524312
  5.2 0.0 copy-start.3
  5.2 1.0 %copy-done.3 = bf16[1,128,2048]{2,1,0:T(8,128)(2,1)S(1)} copy-done((bf16[1,128,2048]{2,1,0:T(8,128)(2,1)S(1)}, bf16[1,128,2048]{2,1,0:T(8,128)(2,1)}, u32[]{:S(2)}) %copy-start.3) | copy-done | bytes 524312
  6.3 29.4 %shard_map.102 = (bf16[128,2048]{1,0:T(8,128)(2,1)S(1)}, bf16[128,2048]{1,0:T(8,128)(2,1)S(1)}, bf16[128,2048]{1,0:T(8,128)(2,1)S(1)}, f32[1,2048]{1,0:T(1,128)S(1)}) custom-call(bf16[128,2048]{1,0:T(8,128)(2,1)S(1)} %bitcast.10, bf16[128,2048]{1,0:T(8,128)(2,1)S(1)} %bitcast.11, bf16[128,2048]{1,0:T(8,128)(2,1)S(1)} %bitcast.12, ...), custom_call_target="tpu_custom_call" | custom-call | tf_op jit(solution)/shard_map/pallas_call | solution.py:272
  35.7 0.8 %copy.16 = bf16[1,128,2048]{2,1,0:T(8,128)(2,1)} copy(bf16[1,128,2048]{2,1,0:T(8,128)(2,1)S(1)} %bitcast.16) | data formatting | bytes 1048576
  36.5 0.8 %copy.17 = bf16[1,128,2048]{2,1,0:T(8,128)(2,1)} copy(bf16[1,128,2048]{2,1,0:T(8,128)(2,1)S(1)} %bitcast.15) | data formatting | bytes 1048576
  37.3 0.8 %copy.18 = bf16[1,128,2048]{2,1,0:T(8,128)(2,1)} copy(bf16[1,128,2048]{2,1,0:T(8,128)(2,1)S(1)} %bitcast.14) | data formatting | bytes 1048576
  38.1 0.6 %copy.19 = f32[2048]{0:T(1024)} copy(f32[2048]{0:T(1024)S(1)} %bitcast.19) | data formatting | bytes 16384
Async XLA Ops:
  0.6 0.7 %copy-start.6 = (bf16[1,128,32]{1,2,0:T(8,128)(2,1)S(1)}, bf16[1,128,32]{1,2,0:T(8,128)(2,1)}, u32[]{:S(2)}) copy-start(bf16[1,128,32]{1,2,0:T(8,128)(2,1)} %param.11) | copy-start | bytes 24580
  1.3 0.7 %copy-start.4 = (f32[2048]{0:T(1024)S(1)}, f32[2048]{0:T(1024)}, u32[]{:S(2)}) copy-start(f32[2048]{0:T(1024)} %param.13) | copy-start | bytes 24580
  1.4 0.7 %copy-start.5 = (s32[1,8]{1,0:T(1,128)S(1)}, s32[1,8]{1,0:T(1,128)}, u32[]{:S(2)}) copy-start(s32[1,8]{1,0:T(1,128)} %doc_ref.1) | copy-start | bytes 100
  2.1 1.0 %copy-start = (bf16[1,128,2048]{2,1,0:T(8,128)(2,1)S(1)}, bf16[1,128,2048]{2,1,0:T(8,128)(2,1)}, u32[]{:S(2)}) copy-start(bf16[1,128,2048]{2,1,0:T(8,128)(2,1)} %param.7) | copy-start | bytes 1572868
  3.2 1.0 %copy-start.1 = (bf16[1,128,2048]{2,1,0:T(8,128)(2,1)S(1)}, bf16[1,128,2048]{2,1,0:T(8,128)(2,1)}, u32[]{:S(2)}) copy-start(bf16[1,128,2048]{2,1,0:T(8,128)(2,1)} %param.8) | copy-start | bytes 1572868
  4.2 1.0 %copy-start.2 = (bf16[1,128,2048]{2,1,0:T(8,128)(2,1)S(1)}, bf16[1,128,2048]{2,1,0:T(8,128)(2,1)}, u32[]{:S(2)}) copy-start(bf16[1,128,2048]{2,1,0:T(8,128)(2,1)} %param.9) | copy-start | bytes 1572868
  5.2 1.0 %copy-start.3 = (bf16[1,128,2048]{2,1,0:T(8,128)(2,1)S(1)}, bf16[1,128,2048]{2,1,0:T(8,128)(2,1)}, u32[]{:S(2)}) copy-start(bf16[1,128,2048]{2,1,0:T(8,128)(2,1)} %param.10) | copy-start | bytes 1572868

commit v2 on v1

--- a/solution.py
+++ b/solution.py
@@ -10,7 +10,7 @@
 
 EPSILON = 1e-05
 MESH = pl.DeviceIdType.MESH
-UNROLL = 4
+UNROLL = 8
 F32 = jnp.float32
 BF16 = jnp.bfloat16
 
@@ -23,21 +23,38 @@
 
 def kernel(
     ctx_count, dp_count, tokens,
-    q_ref, k_ref, v_ref, g_ref, decay_ref, doc_ref, gain_ref,
+    q_hbm, k_hbm, v_hbm, g_hbm, decay_hbm, doc_ref, gain_hbm,
     dq_ref, dk_ref, dv_ref, gain_out_ref,
     rows_s, weight_s, head_s, tail_s, probs_s, attn_s, grad_s, qw_s, dk_s, dv_s,
     carry_all, term_out, term_in, state_out, state_in,
     back_term_out, back_term_in, back_out, back_in,
-    gain_all, gain_mid, gain_dp,
-    send_sem, recv_sem, gain_send_sem, gain_recv_sem,
+    gain_out, gain_in, gain_sum, gain_rows, gain_full,
+    q_ref, k_ref, v_ref, g_ref, decay_ref, gain_ref,
+    send_sem, recv_sem, dp_send_sem, dp_recv_sem, load_sem,
 ):
-    length, width = q_ref.shape
+    length, width = q_hbm.shape
     lanes = 128
     half = lanes // 2
     pairs = width // lanes
     chunk = pairs * half // ctx_count
     me = lax.axis_index("ctx")
     row_me = lax.axis_index("dp")
+
+    loads = [
+        pltpu.make_async_copy(source, target, load_sem.at[i])
+        for i, (source, target) in enumerate(
+            (
+                (decay_hbm, decay_ref),
+                (k_hbm, k_ref),
+                (v_hbm, v_ref),
+                (q_hbm, q_ref),
+                (gain_hbm, gain_ref),
+                (g_hbm, g_ref),
+            )
+        )
+    ]
+    for load in loads:
+        load.start()
 
     barrier = pltpu.get_barrier_semaphore()
     for j in range(1, ctx_count):
@@ -71,7 +88,10 @@
     step_row = lax.broadcasted_iota(jnp.int32, (length, length), 0)
     step_col = lax.broadcasted_iota(jnp.int32, (length, length), 1)
     upto = jnp.where(step_row <= step_col, 1.0, 0.0).astype(BF16)
-    rows_s[...] = dot(decay_ref[...], upto, 0, 0)
+    loads[0].wait()
+    rows_s[...] = dot(decay_ref[...], upto, 1, 0)
+    loads[1].wait()
+    loads[2].wait()
 
     same_doc = doc_ref[0, me] == doc_ref[0, jnp.maximum(me - 1, 0)]
     keep = jnp.where(same_doc, 1.0, 0.0) * jnp.where(me == 0, 0.0, 1.0)
@@ -107,7 +127,7 @@
             copies.append(
                 pltpu.make_async_remote_copy(
                     src_ref=source(other),
-                    dst_ref=target(),
+                    dst_ref=target(other),
                     send_sem=send_sem.at[phase, j],
                     recv_sem=recv_sem.at[phase, j],
                     device_id={"ctx": other},
@@ -138,13 +158,22 @@
 
     def exchange_terms(phase, out_ref, in_ref):
         in_ref[me] = out_ref[piece(me), :]
-        return to_all(phase, lambda other: out_ref.at[piece(other), :], lambda: in_ref.at[me])
+        return to_all(phase, lambda other: out_ref.at[piece(other), :], lambda other: in_ref.at[me])
 
     def exchange_states(phase, out_ref, in_ref):
         in_ref[piece(me), :] = out_ref[me]
-        return to_all(phase, lambda other: out_ref.at[other], lambda: in_ref.at[piece(me), :])
-
-    carry_copies = to_all(0, lambda other: carry_all.at[me], lambda: carry_all.at[me])
+        return to_all(phase, lambda other: out_ref.at[other], lambda other: in_ref.at[piece(me), :])
+
+    owned = max(chunk // half, 1)
+
+    def owner_pairs(index):
+        return pl.ds(lax.div(index * chunk, half), owned)
+
+    carry_copies = to_all(
+        0,
+        lambda other: carry_all.at[me, owner_pairs(other), :],
+        lambda other: carry_all.at[me, owner_pairs(other), :],
+    )
     term_copies = exchange_terms(1, term_out, term_in)
 
     causal = step_row >= step_col
@@ -163,6 +192,7 @@
         qw_s[:, cols(pair)] = (q_ref[:, cols(pair)].astype(F32) * head_s[:, cols(pair)]).astype(BF16)
         return 0
 
+    loads[3].wait()
     over_pairs(0, pairs // 2, local_step)
     finish(carry_copies)
     finish(term_copies)
@@ -179,10 +209,14 @@
         scaled = gain_ref[:, cols(pair)] * g_ref[:, cols(pair)].astype(F32)
         return square + attn * attn, cross + attn * scaled
 
+    loads[4].wait()
+    loads[5].wait()
     zero = jnp.zeros((length, lanes), F32)
     square, cross = over_pairs(0, pairs, attend_step, (zero, zero))
     inv_rms = lax.rsqrt(jnp.sum(square, axis=1, keepdims=True) / width + EPSILON)
     shift = inv_rms * inv_rms * inv_rms * jnp.sum(cross, axis=1, keepdims=True) / width
+
+    share = width // ctx_count
 
     def norm_step(pair, _):
         grad_out = g_ref[:, cols(pair)].astype(F32)
@@ -192,12 +226,19 @@
         grad_s[:, cols(pair)] = grad
         full = dot(qw_s[:, cols(pair)], grad, 0, 0)
         back_term_out[packed_rows(pair), :] = packed(full, half).astype(BF16)
-        gain_all[me, :, cols(pair)] = jnp.sum(grad_out * attn * inv_rms, axis=0, keepdims=True)
+        gain_row = jnp.sum(grad_out * attn * inv_rms, axis=0, keepdims=True)
+        if share < lanes:
+            for i in range(lanes // share):
+                gain_out[pair * (lanes // share) + i] = gain_row[:, i * share : (i + 1) * share]
+        else:
+            per = share // lanes
+            gain_out[lax.div(pair, per), :, cols(lax.rem(pair, per))] = gain_row
         return 0
 
     over_pairs(0, pairs, norm_step)
+    gain_in[me] = gain_out[me]
+    gain_copies = to_all(5, lambda other: gain_out.at[other], lambda other: gain_in.at[me])
     back_term_copies = exchange_terms(3, back_term_out, back_term_in)
-    gain_copies = to_all(4, lambda other: gain_all.at[me], lambda: gain_all.at[me])
 
     def grads_step(pair, _):
         grad = grad_s[:, cols(pair)]
@@ -212,31 +253,38 @@
         return 0
 
     over_pairs(0, pairs // 2, grads_step)
-    finish(back_term_copies)
-    combine(back_term_in, back_out, True)
-    back_copies = exchange_states(5, back_out, back_in)
     finish(gain_copies)
-    gain_ctx = gain_all[0]
+    total = gain_in[0]
     for block in range(1, ctx_count):
-        gain_ctx = gain_ctx + gain_all[block]
-    gain_mid[...] = gain_ctx
+        total = total + gain_in[block]
+    gain_rows[row_me] = total
     dp_copies = []
     for j in range(1, dp_count):
         other = lax.rem(row_me + j, dp_count)
         dp_copies.append(
             pltpu.make_async_remote_copy(
-                src_ref=gain_mid,
-                dst_ref=gain_dp.at[row_me],
-                send_sem=gain_send_sem.at[j],
-                recv_sem=gain_recv_sem.at[j],
+                src_ref=gain_rows.at[row_me],
+                dst_ref=gain_rows.at[row_me],
+                send_sem=dp_send_sem.at[j],
+                recv_sem=dp_recv_sem.at[j],
                 device_id={"dp": other},
                 device_id_type=MESH,
             )
         )
     for copy in dp_copies:
         copy.start()
-    gain_dp[row_me] = gain_ctx
+    finish(back_term_copies)
+    combine(back_term_in, back_out, True)
+    back_copies = exchange_states(4, back_out, back_in)
     over_pairs(pairs // 2, pairs, grads_step)
+    finish(dp_copies)
+    total = gain_rows[0]
+    for row in range(1, dp_count):
+        total = total + gain_rows[row]
+    total = total / math.sqrt(tokens)
+    gain_sum[...] = total
+    gain_full[me] = total
+    full_copies = to_all(6, lambda other: gain_sum, lambda other: gain_full.at[me])
     finish(back_copies)
 
     def last_step(pair, _):
@@ -249,11 +297,21 @@
         return 0
 
     over_pairs(0, pairs, last_step)
-    finish(dp_copies)
-    gain_total = gain_dp[0]
-    for row in range(1, dp_count):
-        gain_total = gain_total + gain_dp[row]
-    gain_out_ref[...] = gain_total / math.sqrt(tokens)
+    finish(full_copies)
+    for block in range(ctx_count):
+        gain_out_ref[:, block * share : (block + 1) * share] = gain_full[block]
+
+
+def write_out(*refs):
+    sources, targets, sem = refs[:4], refs[4:8], refs[8]
+    copies = [
+        pltpu.make_async_copy(source, target, sem.at[i])
+        for i, (source, target) in enumerate(zip(sources, targets))
+    ]
+    for copy in copies:
+        copy.start()
+    for copy in copies:
+        copy.wait()
 
 
 def body(query_in, key_in, value_in, out_grad, log_decay, doc_ids, norm_gain):
@@ -269,10 +327,14 @@
     wide, narrow = pltpu.VMEM((length, width), F32), pltpu.VMEM((length, width), BF16)
     whole_state = pltpu.VMEM((pairs * 64, lanes), BF16)
     pieces = pltpu.VMEM((ctx_count, chunk, lanes), BF16)
-    dq, dk, dv, gain_grad = pl.pallas_call(
+    anywhere = pl.BlockSpec(memory_space=pl.ANY)
+    outs = (flat, flat, flat, jax.ShapeDtypeStruct((1, width), F32))
+    gain_share = width // ctx_count
+    gain_pieces = pltpu.VMEM((ctx_count, 1, gain_share), F32)
+    results = pl.pallas_call(
         functools.partial(kernel, ctx_count, dp_count, tokens),
-        out_shape=(flat, flat, flat, jax.ShapeDtypeStruct((1, width), F32)),
-        in_specs=[vmem] * 5 + [pl.BlockSpec(memory_space=pltpu.SMEM), vmem],
+        out_shape=outs,
+        in_specs=[anywhere] * 5 + [pl.BlockSpec(memory_space=pltpu.SMEM), anywhere],
         out_specs=(vmem,) * 4,
         scratch_shapes=[
             pltpu.VMEM((heads, length), F32),
@@ -294,21 +356,38 @@
             pieces,
             pieces,
             whole_state,
-            pltpu.VMEM((ctx_count, 1, width), F32),
+            gain_pieces,
+            gain_pieces,
+            pltpu.VMEM((1, gain_share), F32),
+            pltpu.VMEM((dp_count, 1, gain_share), F32),
+            gain_pieces,
+            narrow,
+            narrow,
+            narrow,
+            narrow,
+            pltpu.VMEM((heads, length), BF16),
             pltpu.VMEM((1, width), F32),
-            pltpu.VMEM((dp_count, 1, width), F32),
-            pltpu.SemaphoreType.DMA((6, ctx_count)),
-            pltpu.SemaphoreType.DMA((6, ctx_count)),
+            pltpu.SemaphoreType.DMA((7, ctx_count)),
+            pltpu.SemaphoreType.DMA((7, ctx_count)),
             pltpu.SemaphoreType.DMA((dp_count,)),
             pltpu.SemaphoreType.DMA((dp_count,)),
+            pltpu.SemaphoreType.DMA((6,)),
         ],
         compiler_params=pltpu.CompilerParams(
-            collective_id=0, has_side_effects=True, vmem_limit_bytes=40 * 1024 * 1024
+            collective_id=0, has_side_effects=True, vmem_limit_bytes=56 * 1024 * 1024
         ),
     )(
-        query_in[0], key_in[0], value_in[0], out_grad[0], log_decay[0], doc_ids,
+        query_in[0], key_in[0], value_in[0], out_grad[0], log_decay[0].T, doc_ids,
         norm_gain.reshape(1, width),
     )
+    dq, dk, dv, gain_grad = pl.pallas_call(
+        write_out,
+        out_shape=outs,
+        in_specs=[vmem] * 4,
+        out_specs=(anywhere,) * 4,
+        scratch_shapes=[pltpu.SemaphoreType.DMA((4,))],
+        compiler_params=pltpu.CompilerParams(vmem_limit_bytes=56 * 1024 * 1024),
+    )(*results)
     return dq[None], dk[None], dv[None], gain_grad[0]
 
 

time: 39.1 us -> 33.2 us (0.85)
  local copies, waits for them, and re-layouts: 8.61 us -> 0 us
  Pallas kernels: 29.4 us -> 32.3 us
    unnamed x19 -> x0, local copies, waits for them, and re-layouts: 8.61 us -> none
    pallas_call x0 -> x1, Pallas kernels: none -> 2.54 us  [body(): pl.pallas_call(write_out, out_shape=outs, in_specs=[vmem] * 4, out_specs=...]
    pallas_call x1, Pallas kernels: 29.4 us -> 29.8 us  [body(): pl.pallas_call(functools.partial(kernel, ctx_count, dp_count, tokens), ou...]
where the time goes in v2:
time: 33.2 us; the launch traced here: 33 us
  Pallas kernels  32.3 us (97%)
  between operations  0.64 us (2%)
    pallas_call x1, Pallas kernels, body(): pl.pallas_call(functools.partial(kernel, ctx_count, dp_count, tokens), ou...  29.8 us
    pallas_call x1, Pallas kernels, body(): pl.pallas_call(write_out, out_shape=outs, in_specs=[vmem] * 4, out_specs=...  2.54 us

profile of v2, /device:TPU:0, one launch (start us, length us, event | category | flops | bytes accessed | tf_op | source)
XLA Modules:
  0.0 33.0 jit_solution(9152684397242522157)
XLA Ops:
  0.6 29.8 %shard_map.102 = (bf16[128,2048]{1,0:T(8,128)(2,1)}, bf16[128,2048]{1,0:T(8,128)(2,1)}, bf16[128,2048]{1,0:T(8,128)(2,1)}, f32[1,2048]{1,0:T(1,128)}) custom-call(bf16[128,2048]{1,0:T(8,128)(2,1)} %bitcast.12, bf16[128,2048]{1,0:T(8,128)(2,1)} %bitcast.13, bf16[128,2048]{1,0:T(8,128)(2,1)} %bitcast.14, bf16[128,2048]{1,0:T(8,128)(2,1)} %bitcast.15, ...), custom_call_target="tpu_custom_call" | custom-call | tf_op jit(solution)/shard_map/pallas_call | solution.py:334
  30.5 2.5 %shard_map.103 = (bf16[128,2048]{1,0:T(8,128)(2,1)}, bf16[128,2048]{1,0:T(8,128)(2,1)}, bf16[128,2048]{1,0:T(8,128)(2,1)}, f32[1,2048]{1,0:T(1,128)}) custom-call(bf16[128,2048]{1,0:T(8,128)(2,1)} %get-tuple-element.12.refs_0_, bf16[128,2048]{1,0:T(8,128)(2,1)} %get-tuple-element.13.refs_1_, bf16[128,2048]{1,0:T(8,128)(2,1)} %get-tuple-element.14.refs_2_, ...), custom_call_target="tpu_custom_call" | custom-call | tf_op jit(solution)/shard_map/pallas_call | solution.py:383

commit v3 on v2

--- a/solution.py
+++ b/solution.py
@@ -303,15 +303,26 @@
 
 
 def write_out(*refs):
-    sources, targets, sem = refs[:4], refs[4:8], refs[8]
-    copies = [
-        pltpu.make_async_copy(source, target, sem.at[i])
-        for i, (source, target) in enumerate(zip(sources, targets))
-    ]
-    for copy in copies:
-        copy.start()
-    for copy in copies:
-        copy.wait()
+    sources, targets, staged, in_sem, out_sem = refs[:4], refs[4:8], refs[8:12], refs[12], refs[13]
+    moves = []
+    for source, target, stage in zip(sources, targets, staged):
+        count = source.shape[0]
+        step = max(count // 2, 1)
+        for first in range(0, count, step):
+            rows, i = pl.ds(first, step), len(moves)
+            moves.append(
+                (
+                    pltpu.make_async_copy(source.at[rows, :], stage.at[rows, :], in_sem.at[i]),
+                    pltpu.make_async_copy(stage.at[rows, :], target.at[rows, :], out_sem.at[i]),
+                )
+            )
+    for load, _ in moves:
+        load.start()
+    for load, store in moves:
+        load.wait()
+        store.start()
+    for _, store in moves:
+        store.wait()
 
 
 def body(query_in, key_in, value_in, out_grad, log_decay, doc_ids, norm_gain):
@@ -383,9 +394,11 @@
     dq, dk, dv, gain_grad = pl.pallas_call(
         write_out,
         out_shape=outs,
-        in_specs=[vmem] * 4,
+        in_specs=[anywhere] * 4,
         out_specs=(anywhere,) * 4,
-        scratch_shapes=[pltpu.SemaphoreType.DMA((4,))],
+        scratch_shapes=[narrow] * 3
+        + [pltpu.VMEM((1, width), F32)]
+        + [pltpu.SemaphoreType.DMA((7,))] * 2,
         compiler_params=pltpu.CompilerParams(vmem_limit_bytes=56 * 1024 * 1024),
     )(*results)
     return dq[None], dk[None], dv[None], gain_grad[0]

time: 33.2 us -> 32.9 us (level)
  no operation moved by 1% of the time
where the time goes in v3:
time: 32.9 us; the launch traced here: 32.7 us
  Pallas kernels  32 us (97%)
  between operations  0.64 us (2%)
    pallas_call x1, Pallas kernels, body(): pl.pallas_call(functools.partial(kernel, ctx_count, dp_count, tokens), ou...  29.8 us
    pallas_call x1, Pallas kernels, body(): pl.pallas_call(write_out, out_shape=outs, in_specs=[anywhere] * 4, out_sp...  2.21 us

profile of v3, /device:TPU:0, one launch (start us, length us, event | category | flops | bytes accessed | tf_op | source)
XLA Modules:
  0.0 32.7 jit_solution(11821533187814818199)
XLA Ops:
  0.6 29.8 %shard_map.102 = (bf16[128,2048]{1,0:T(8,128)(2,1)}, bf16[128,2048]{1,0:T(8,128)(2,1)}, bf16[128,2048]{1,0:T(8,128)(2,1)}, f32[1,2048]{1,0:T(1,128)}) custom-call(bf16[128,2048]{1,0:T(8,128)(2,1)} %bitcast.12, bf16[128,2048]{1,0:T(8,128)(2,1)} %bitcast.13, bf16[128,2048]{1,0:T(8,128)(2,1)} %bitcast.14, bf16[128,2048]{1,0:T(8,128)(2,1)} %bitcast.15, ...), custom_call_target="tpu_custom_call" | custom-call | tf_op jit(solution)/shard_map/pallas_call | solution.py:345
  30.5 2.2 %shard_map.103 = (bf16[128,2048]{1,0:T(8,128)(2,1)}, bf16[128,2048]{1,0:T(8,128)(2,1)}, bf16[128,2048]{1,0:T(8,128)(2,1)}, f32[1,2048]{1,0:T(1,128)}) custom-call(bf16[128,2048]{1,0:T(8,128)(2,1)} %get-tuple-element.12.refs_0_, bf16[128,2048]{1,0:T(8,128)(2,1)} %get-tuple-element.13.refs_1_, bf16[128,2048]{1,0:T(8,128)(2,1)} %get-tuple-element.14.refs_2_, ...), custom_call_target="tpu_custom_call" | custom-call | tf_op jit(solution)/shard_map/pallas_call | solution.py:394
